TPU v7x, 32 devices: a whole 2x2x4 slice. The times are simulated.
32 devices in a mesh: groups: 2 (over y), row: 4 (over z), col: 4 (over x, core).
Axes of the slice: x: 2, y: 2, z: 4, core: 2. Of those that a mesh axis runs over, the one named last changes fastest.
Arguments:
- values: float32 [1024, 4, 128, 128], P(('groups', 'row'), 'col'), parts along dimension 0, as said below
- partner: int32 [1024, 4], P(('groups', 'row'), 'col'), parts along dimension 0, may hold values from 0 to 511, as said below
Outputs:
- product: float32 [1024, 4, 128, 128], P(('groups', 'row'), 'col'), parts along dimension 0
There are 2 independent parts, one for each index of `groups`. A program takes and returns all parts, laid end to end along the dimension named above; each array names one. Nothing has to cross between parts.
Inputs may be any that keep to these rules, and one draw needn't show every extreme that they name: partner[i, c] lies in column range c, that is c * 128 <= partner[i, c] < (c + 1) * 128; partner[i, i // 128] = i; the pattern is symmetric: partner[partner[i, c], i // 128] = i. values[i, c] is the transpose of values[partner[i, c], i // 128], so X is symmetric.
All inputs are finite; a program needn't handle non-finite values.
Results may differ from a plain program's by a relative error of at most 0.0003.
Values sent between devices are 32-bit elements; how exact they have to be, the bound alone decides.
A program may use at most 192 MiB of HBM per device.

v0:
```python
import jax
import jax.numpy as jnp
from jax import lax
from jax.sharding import PartitionSpec as P

STEPS = 3


def passed_along(value, axis, steps):
    count = lax.axis_size(axis)
    pairs = [(source, (source + steps) % count) for source in range(count)]
    return lax.ppermute(value, axis, pairs)


def spread(value, axis, root):
    mine = lax.axis_index(axis) == root
    return lax.psum(jnp.where(mine, value, jnp.zeros_like(value)), axis)


def per_device(values, partner):
    rows_tile = values.shape[0]
    col_count = lax.axis_size("col")
    range_count = col_count // lax.axis_size("row")
    range_size = rows_tile // range_count
    column = lax.axis_index("col")
    own_block = values[:, 0]
    own_cols = partner[:, 0]
    accumulated = jnp.zeros(own_block.shape, jnp.float32)
    carried_block = own_block
    carried_cols = own_cols
    for window in range(STEPS):
        if window > 0:
            carried_block, carried_cols = passed_along(
                (carried_block, carried_cols), "col", col_count - 1
            )
        target_range = (column + window) % col_count
        source_row = target_range // range_count
        part_index = target_range % range_count
        mine_block = lax.dynamic_slice_in_dim(own_block, part_index * range_size, range_size, 0)
        mine_cols = lax.dynamic_slice_in_dim(own_cols, part_index * range_size, range_size, 0)
        right_block, right_cols = (
            spread(mine_block, "row", source_row),
            spread(mine_cols, "row", source_row),
        )
        offsets = carried_cols - target_range * range_size
        gathered = jnp.take(right_block, offsets, axis=0)
        reached = jnp.take(right_cols, offsets, axis=0)
        product = jnp.einsum(
            "nxy,nyz->nxz",
            carried_block,
            gathered,
            precision=lax.Precision.HIGHEST,
            preferred_element_type=jnp.float32,
        )
        accumulated = accumulated + jnp.where((reached == own_cols)[:, None, None], product, 0.0)
    return accumulated[:, None]


def solution(mesh):
    return jax.shard_map(
        per_device,
        mesh=mesh,
        in_specs=(P(("groups", "row"), "col", None, None), P(("groups", "row"), "col")),
        out_specs=P(("groups", "row"), "col", None, None),
        check_vma=False,
    )
```

profile of v0, /device:TPU:25, one launch (start us, length us, event | category | flops | bytes accessed | tf_op | source)
XLA Modules:
  0.0 955.1 jit_solution(14324051470699343946)
XLA Ops:
  6.5 0.0 all-reduce.4.cloned.1.call-start
  6.5 11.2 %broadcast_select_fusion.1 = (f32[128,128,128]{2,1,0:T(8,128)}, f32[128,128,128]{2,1,0:T(8,128)}, f32[128,128,128]{2,1,0:T(8,128)}) fusion(pred[]{:T(512)S(6)} %eq.32, f32[128,1,128,128]{3,2,1,0:T(8,128)} %param.6, pred[]{:T(512)S(6)} %eq.28, pred[]{:T(512)S(6)} %eq.30), kind=kLoop, calls=%fused_computation.17 | loop fusion | flops 6291456 | bytes 33554436 | tf_op jit(solution)/shard_map/jit(_where)/select_n | solution.py:17
  17.7 0.0 all-reduce.4.cloned.1.call-update
  17.7 0.7 collective-permute-start.1
  18.5 92.8 %collective-permute-done.1 = f32[128,128,128]{2,1,0:T(8,128)} collective-permute-done((f32[128,128,128]{2,1,0:T(8,128)}, f32[128,128,128]{2,1,0:T(8,128)}, u32[]{:S(2)}, u32[]{:S(2)}) %collective-permute-start.1) | collective-permute-done | bytes 8388640 | tf_op jit(solution)/shard_map/ppermute | solution.py:12
  111.3 0.0 collective-permute-start.3
  111.3 0.0 copy-done.1
  111.3 1.6 collective-permute-start
  112.9 7.3 all-reduce
  120.2 1.2 gather_fusion
  121.4 83.4 %collective-permute-done = s32[128]{0:T(128)S(1)} collective-permute-done((s32[128]{0:T(128)S(1)}, s32[128]{0:T(128)S(1)}, u32[]{:S(2)}, u32[]{:S(2)}) %collective-permute-start) | collective-permute-done | bytes 544 | tf_op jit(solution)/shard_map/ppermute | solution.py:12
  204.8 0.0 collective-permute-start.2
  204.8 1.2 gather_fusion.2
  206.0 2.1 collective-permute-done.2
  208.2 1.2 gather_fusion.4
  209.4 643.0 %all-reduce.4.cloned.1.call-done = (f32[128,128,128]{2,1,0:T(8,128)}, f32[128,128,128]{2,1,0:T(8,128)}, f32[128,128,128]{2,1,0:T(8,128)}) async-done(((f32[128,128,128]{2,1,0:T(8,128)}, f32[128,128,128]{2,1,0:T(8,128)}, f32[128,128,128]{2,1,0:T(8,128)}), (f32[128,128,128]{2,1,0:T(8,128)}, f32[128,128,128]{2,1,0:T(8,128)}, f32[128,128,128]{2,1,0:T(8,128)})) %all-reduce.4.cloned.1.call-update) | async-done | bytes 25165840 | tf_op jit(solution)/shard_map/psum | solution.py:17
  852.4 7.7 gather_fusion.1
  860.1 7.9 gather_fusion.3
  868.0 7.7 gather_fusion.5
  875.6 21.4 %fusion.4 = f32[128,128,128]{2,1,0:T(8,128)} fusion(f32[128,128,128]{2,1,0:T(8,128)} %gather_fusion.1, pred[128]{0:T(512)(128)(4,1)S(1)} %get-tuple-element.15, f32[128,1,128,128]{3,2,1,0:T(8,128)} %param.6), kind=kOutput, calls=%fused_computation.10 | convolution fusion | flops 3223322624 | bytes 25165952 | tf_op jit(solution)/shard_map/nxy,nyz->nxz/dot_general | solution.py:48
  897.0 17.9 %fusion.2 = f32[128,128,128]{2,1,0:T(8,128)} fusion(f32[128,128,128]{2,1,0:T(8,128)} %collective-permute-done.1, f32[128,128,128]{2,1,0:T(8,128)S(1)} %copy-done, pred[128]{0:T(512)(128)(4,1)S(1)} %get-tuple-element.17), kind=kOutput, calls=%fused_computation.8 | convolution fusion | flops 3223322624 | bytes 25165952 | tf_op jit(solution)/shard_map/nxy,nyz->nxz/dot_general | solution.py:48
  914.9 0.0 collective-permute-done.3
  914.9 24.3 %add_bitcast_fusion = f32[128,1,128,128]{2,3,0,1:T(8,128)} fusion(f32[128,128,128]{2,1,0:T(8,128)} %fusion.2, f32[128,128,128]{2,1,0:T(8,128)} %fusion.4, pred[128]{0:T(512)(128)(4,1)S(1)} %get-tuple-element.24, pred[128]{0:T(512)(128)(4,1)S(1)} %get-tuple-element.23, pred[128]{0:T(512)(128)(4,1)S(1)} %get-tuple-element.22, ...), kind=kOutput, calls=%fused_computation.12 | convolution fusion | flops 3233808384 | bytes 41943552 | tf_op jit(solution)/shard_map/nxy,nyz->nxz/dot_general | solution.py:48
  939.3 9.0 copy.10
  (11 shorter events, 0.1 us)
Async XLA Ops:
  6.5 845.9 %all-reduce.4.cloned.1.call-start = ((), (), s32[]{:S(2)}) async-start(), calls=%async_computation | async-start | bytes 50331648 | tf_op jit(solution)/shard_map/psum | solution.py:17
  17.7 93.6 %copy-start.1 = (s32[128,1]{0,1:T(1,128)S(1)}, s32[128,1]{0,1:T(1,128)}, u32[]{:S(2)}) copy-start(s32[128,1]{0,1:T(1,128)} %param.7) | copy-start | bytes 1540
  17.7 93.6 %collective-permute-start.1 = (f32[128,128,128]{2,1,0:T(8,128)}, f32[128,128,128]{2,1,0:T(8,128)}, u32[]{:S(2)}, u32[]{:S(2)}) collective-permute-start(f32[128,128,128]{2,1,0:T(8,128)} %bitcast.21), channel_id=1, source_target_pairs={{0,3},{1,0},{2,1},{3,2},{4,7},{5,4},{6,5},{7,6},{8,11},{9,8},{10,9... | collective-permute-start | bytes 25165832 | tf_op jit(solution)/shard_map/ppermute | solution.py:12
  111.3 803.6 %collective-permute-start.3 = (f32[128,128,128]{2,1,0:T(8,128)}, f32[128,128,128]{2,1,0:T(8,128)}, u32[]{:S(2)}, u32[]{:S(2)}) collective-permute-start(f32[128,128,128]{2,1,0:T(8,128)} %collective-permute-done.1), channel_id=1, source_target_pairs={{0,3},{1,0},{2,1},{3,2},{4,7},{5,4},{6,5},{7,6},{8,11},{9,8},{10,9... | collective-permute-start | bytes 25165832 | tf_op jit(solution)/shard_map/ppermute | solution.py:12
  111.3 93.5 %collective-permute-start = (s32[128]{0:T(128)S(1)}, s32[128]{0:T(128)S(1)}, u32[]{:S(2)}, u32[]{:S(2)}) collective-permute-start(s32[128]{0:T(128)S(1)} %bitcast.22), channel_id=1, source_target_pairs={{0,3},{1,0},{2,1},{3,2},{4,7},{5,4},{6,5},{7,6},{8,11},{9,8},{10,9... | collective-permute-start | bytes 1544 | tf_op jit(solution)/shard_map/ppermute | solution.py:12
  204.8 3.4 collective-permute-start.2
  875.6 21.4 %copy-start = (f32[128,128,128]{2,1,0:T(8,128)S(1)}, f32[128,128,128]{2,1,0:T(8,128)}, u32[]{:S(2)}) copy-start(f32[128,128,128]{2,1,0:T(8,128)} %gather_fusion.3) | copy-start | bytes 25165828
Sparse Core Ops, SparseCore 0:
  17.8 834.5 all-reduce.3
where the time goes:
time: 959 us; the launch traced here: 955 us
  waiting for transfers between devices  821 us (86%)
  matrix products  63.6 us (7%)
  local copies, waits for them, and re-layouts  35.9 us (4%)
  between operations  13.5 us (1%)
  other arithmetic  11.2 us (1%)
    psum x1, waiting for transfers between devices, spread(): return lax.psum(jnp.where(mine, value, jnp.zeros_like(value)), axis)  643 us
    ppermute x4, waiting for transfers between devices, passed_along(): return lax.ppermute(value, axis, pairs)  178 us
    dot_general x3, matrix products, per_device(): jnp.einsum('nxy,nyz->nxz', carried_block, gathered, precision=lax.Precisi...  63.6 us
    gather x3, local copies, waits for them, and re-layouts, per_device(): gathered = jnp.take(right_block, offsets, axis=0)  23.2 us
  transfers between devices with their start and end apart: 5, of which 4 were waited for; matrix products, arithmetic and copies ran while one was open for 7% of the time, Pallas kernels for 0%

commit v1 on v0

--- a/solution.py
+++ b/solution.py
@@ -1,9 +1,343 @@
+import functools
 import jax
 import jax.numpy as jnp
 from jax import lax
+from jax.experimental import pallas as pl
+from jax.experimental.pallas import tpu as pltpu
 from jax.sharding import PartitionSpec as P
 
 STEPS = 3
+MESH = pl.DeviceIdType.MESH
+SIDE = 4
+CHUNKS = 8
+GROUP = 4
+
+FLOWS = (
+    (0, 0, 0, 1, 0, 1, 0),
+    (0, 0, 0, 2, 0, 1, 1),
+    (0, 1, 0, 2, 0, 2, 0),
+    (0, 1, 0, 3, 0, 3, 0),
+    (0, 1, 1, 1, 1, 1, 0),
+    (0, 1, 1, 2, 1, 1, 1),
+    (0, 1, 3, 1, 2, 1, 1),
+    (0, 2, 0, 3, 0, 3, 0),
+    (0, 2, 0, 0, 0, 0, 0),
+    (0, 2, 2, 2, 1, 2, 1),
+    (0, 2, 2, 3, 1, 2, 1),
+    (0, 3, 0, 0, 0, 2, 1),
+    (0, 3, 0, 1, 0, 1, 0),
+    (0, 3, 3, 3, 1, 3, 2),
+    (0, 3, 3, 1, 0, 1, 2),
+    (1, 0, 1, 1, 1, 1, 0),
+    (1, 0, 1, 2, 1, 1, 1),
+    (1, 0, 0, 0, 0, 0, 0),
+    (1, 0, 2, 0, 2, 0, 0),
+    (1, 1, 1, 2, 1, 2, 0),
+    (1, 1, 1, 3, 1, 2, 1),
+    (1, 2, 1, 3, 1, 3, 0),
+    (1, 2, 1, 0, 1, 0, 0),
+    (1, 2, 2, 2, 2, 2, 0),
+    (1, 2, 2, 3, 2, 3, 0),
+    (1, 2, 0, 2, 0, 2, 0),
+    (1, 3, 1, 0, 1, 2, 1),
+    (1, 3, 1, 1, 1, 1, 0),
+    (1, 3, 3, 3, 2, 3, 1),
+    (1, 3, 0, 3, 0, 2, 1),
+    (2, 0, 2, 1, 2, 1, 0),
+    (2, 0, 2, 2, 2, 1, 1),
+    (2, 0, 0, 0, 1, 0, 1),
+    (2, 0, 0, 1, 3, 0, 1),
+    (2, 1, 2, 2, 2, 2, 0),
+    (2, 1, 2, 3, 2, 3, 0),
+    (2, 1, 1, 1, 1, 0, 1),
+    (2, 1, 3, 1, 3, 1, 0),
+    (2, 2, 2, 3, 2, 3, 0),
+    (2, 2, 2, 0, 2, 3, 1),
+    (2, 3, 2, 0, 2, 0, 0),
+    (2, 3, 2, 1, 2, 1, 0),
+    (2, 3, 3, 3, 3, 3, 0),
+    (2, 3, 3, 0, 3, 2, 2),
+    (2, 3, 1, 3, 1, 3, 0),
+    (3, 0, 3, 1, 3, 1, 0),
+    (3, 0, 3, 2, 3, 1, 1),
+    (3, 0, 0, 0, 2, 0, 2),
+    (3, 0, 0, 1, 0, 1, 0),
+    (3, 0, 2, 0, 3, 2, 2),
+    (3, 1, 3, 2, 3, 2, 0),
+    (3, 1, 3, 3, 3, 3, 0),
+    (3, 1, 1, 1, 2, 1, 2),
+    (3, 1, 2, 1, 2, 1, 0),
+    (3, 2, 3, 3, 3, 3, 0),
+    (3, 2, 3, 0, 3, 3, 1),
+    (3, 2, 2, 2, 2, 2, 0),
+    (3, 2, 2, 0, 2, 3, 1),
+    (3, 3, 3, 0, 3, 0, 0),
+    (3, 3, 3, 1, 3, 1, 0),
+)
+
+
+def plan():
+    devices = [(r, c) for r in range(SIDE) for c in range(SIDE)]
+    forwarded = {(s, p) for _, p, s, _ in split_flows() if s != p}
+    slots = {}
+    for device in devices:
+        arriving = [(p, hops) for d, p, _, hops in split_flows() if d == device]
+        arriving.sort(key=lambda item: ((device, item[0]) not in forwarded, item[1]))
+        slots[device] = {device: 0}
+        for slot, (panel, _) in enumerate(arriving):
+            slots[device][panel] = slot + 1
+    slot_count = max(len(held) for held in slots.values())
+    sends = {device: [] for device in devices}
+    forwards = {device: [[] for _ in range(slot_count)] for device in devices}
+    senders = {device: [None] * slot_count for device in devices}
+    for receiver, panel, sender, _ in split_flows():
+        target = (slots[receiver][panel], receiver)
+        senders[receiver][target[0]] = sender
+        if sender == panel:
+            sends[sender].append(target)
+        else:
+            forwards[sender][slots[sender][panel]].append(target)
+    return devices, slots, slot_count, sends, forwards, senders
+
+
+def split_flows():
+    return [((a, b), (c, d), (e, f), hops) for a, b, c, d, e, f, hops in FLOWS]
+
+
+def encoded(target):
+    return -1 if target is None else (target[0] * SIDE + target[1][0]) * SIDE + target[1][1]
+
+
+def picked(me, table):
+    value = jnp.int32(table[0])
+    for position in range(1, len(table)):
+        if table[position] != table[0]:
+            value = jnp.where(me == position, jnp.int32(table[position]), value)
+    return value
+
+
+def padded(items, count):
+    return list(items) + [None] * (count - len(items))
+
+
+def transport_kernel(own_ref, held_ref, send_sem, recv_sem, own_sem):
+    devices, _, slot_count, sends, forwards, senders = plan()
+    group, row, col = lax.axis_index("groups"), lax.axis_index("row"), lax.axis_index("col")
+    me = row * SIDE + col
+    send_count = max(len(sends[d]) for d in devices)
+    fan = [max(len(forwards[d][slot]) for d in devices) for slot in range(slot_count)]
+    chunk = own_ref.shape[0] // CHUNKS
+
+    def table(entry):
+        return picked(me, [encoded(entry(d)) for d in devices])
+
+    send_codes = [table(lambda d: padded(sends[d], send_count)[k]) for k in range(send_count)]
+    forward_codes = [
+        [table(lambda d: padded(forwards[d][slot], fan[slot])[k]) for k in range(fan[slot])]
+        for slot in range(slot_count)
+    ]
+    sender_codes = [
+        table(lambda d: None if senders[d][slot] is None else (0, senders[d][slot]))
+        for slot in range(slot_count)
+    ]
+    all_codes = send_codes + [code for codes in forward_codes for code in codes]
+
+    def place(code):
+        return (group, code // SIDE % SIDE, code % SIDE)
+
+    barrier = pltpu.get_barrier_semaphore()
+    for slot in range(1, slot_count):
+        @pl.when(sender_codes[slot] >= 0)
+        def _():
+            pl.semaphore_signal(
+                barrier, inc=1, device_id=place(sender_codes[slot]), device_id_type=MESH
+            )
+    receivers = [len(sends[d]) + sum(len(targets) for targets in forwards[d]) for d in devices]
+    pl.semaphore_wait(barrier, picked(me, receivers))
+
+    own_copy = pltpu.make_async_copy(own_ref, held_ref.at[0], own_sem)
+
+    def piece(q):
+        return pl.ds(q * chunk, chunk)
+
+    def moved(source, code, index, q):
+        slot = code // (SIDE * SIDE)
+        return pltpu.make_async_remote_copy(
+            src_ref=source,
+            dst_ref=held_ref.at[slot, piece(q)],
+            send_sem=send_sem.at[index, q],
+            recv_sem=recv_sem.at[slot, q],
+            device_id=place(code),
+            device_id_type=MESH,
+        )
+
+    def arrived(slot, q):
+        pltpu.make_async_remote_copy(
+            src_ref=held_ref.at[slot, piece(q)],
+            dst_ref=held_ref.at[slot, piece(q)],
+            send_sem=send_sem.at[0, q],
+            recv_sem=recv_sem.at[slot, q],
+            device_id=place(sender_codes[slot]),
+            device_id_type=MESH,
+        ).wait_recv()
+
+    def start_own(q, carry):
+        for index, code in enumerate(send_codes):
+            @pl.when(code >= 0)
+            def _():
+                moved(own_ref.at[piece(q)], code, index, q).start()
+        return carry
+
+    lax.fori_loop(0, CHUNKS, start_own, 0)
+    own_copy.start()
+
+    def pass_on(q, carry):
+        index = send_count
+        for slot in range(1, slot_count):
+            if not fan[slot]:
+                continue
+
+            @pl.when(forward_codes[slot][0] >= 0)
+            def _():
+                arrived(slot, q)
+            for code in forward_codes[slot]:
+                @pl.when(code >= 0)
+                def _():
+                    moved(held_ref.at[slot, piece(q)], code, index, q).start()
+                index += 1
+        return carry
+
+    lax.fori_loop(0, CHUNKS, pass_on, 0)
+
+    def finish(q, carry):
+        for slot in range(1, slot_count):
+            waits = sender_codes[slot] >= 0
+            if fan[slot]:
+                waits = jnp.logical_and(waits, forward_codes[slot][0] < 0)
+
+            @pl.when(waits)
+            def _():
+                arrived(slot, q)
+        for index, code in enumerate(all_codes):
+            @pl.when(code >= 0)
+            def _():
+                moved(own_ref.at[piece(q)], code, index, q).wait_send()
+        return carry
+
+    lax.fori_loop(0, CHUNKS, finish, 0)
+    own_copy.wait()
+
+
+def transported(own_block):
+    devices, _, slot_count, sends, forwards, _ = plan()
+    copies = max(len(sends[d]) for d in devices) + sum(
+        max(len(forwards[d][slot]) for d in devices) for slot in range(slot_count)
+    )
+    return pl.pallas_call(
+        transport_kernel,
+        out_shape=jax.ShapeDtypeStruct((slot_count,) + own_block.shape, own_block.dtype),
+        in_specs=[pl.BlockSpec(memory_space=pl.ANY)],
+        out_specs=pl.BlockSpec(memory_space=pl.ANY),
+        scratch_shapes=[
+            pltpu.SemaphoreType.DMA((copies, CHUNKS)),
+            pltpu.SemaphoreType.DMA((slot_count, CHUNKS)),
+            pltpu.SemaphoreType.DMA,
+        ],
+        compiler_params=pltpu.CompilerParams(collective_id=0, has_side_effects=True),
+        name="transport",
+    )(own_block)
+
+
+def column_at(table, row_range, col_range, size, position):
+    return table[(row_range * SIDE + col_range) * size + position]
+
+
+def halves(block):
+    high = block.astype(jnp.bfloat16)
+    return high, (block - high.astype(jnp.float32)).astype(jnp.bfloat16)
+
+
+def product_kernel(size, meta, table, *refs):
+    lefts = refs[:STEPS]
+    rights = refs[STEPS : STEPS + STEPS * GROUP]
+    out_ref = refs[-1]
+    row, col = meta[0], meta[1]
+    for member in range(GROUP):
+        position = pl.program_id(0) * GROUP + member
+        target = column_at(table, row, col, size, position)
+        left_parts, right_parts = [], []
+        for window in range(STEPS):
+            between = lax.rem(col + window, SIDE)
+            reach = column_at(table, row, between, size, position) - between * size
+            reached = column_at(table, between, col, size, reach)
+            left_high, left_low = halves(lefts[window][0, member])
+            block = rights[window * GROUP + member][0, 0]
+            block = lax.cond(meta[8 + window] > 0, lambda b: b.T, lambda b: b, block)
+            block = jnp.where(reached == target, block, 0.0)
+            right_high, right_low = halves(block)
+            left_parts += [left_high, left_low, left_high]
+            right_parts += [right_high, right_high, right_low]
+        out_ref[member] = jnp.dot(
+            jnp.concatenate(left_parts, axis=1),
+            jnp.concatenate(right_parts, axis=0),
+            preferred_element_type=jnp.float32,
+        )
+
+
+def multiplied(held, meta, table):
+    size, width = held.shape[1], held.shape[2]
+
+    def left_spec(window):
+        return pl.BlockSpec(
+            (1, GROUP, width, width), lambda i, meta, table: (meta[2 + window], i, 0, 0)
+        )
+
+    def right_spec(window, member):
+        def index_map(i, meta, table):
+            row, col = meta[0], meta[1]
+            between = lax.rem(col + window, SIDE)
+            other = jnp.where(meta[8 + window] > 0, col, between)
+            place = column_at(table, row, other, size, i * GROUP + member) - other * size
+            return meta[5 + window], place, 0, 0
+
+        return pl.BlockSpec((1, 1, width, width), index_map)
+
+    specs = [left_spec(w) for w in range(STEPS)]
+    specs += [right_spec(w, m) for w in range(STEPS) for m in range(GROUP)]
+    return pl.pallas_call(
+        functools.partial(product_kernel, size),
+        out_shape=jax.ShapeDtypeStruct((size, width, width), jnp.float32),
+        grid_spec=pltpu.PrefetchScalarGridSpec(
+            num_scalar_prefetch=2,
+            grid=(size // GROUP,),
+            in_specs=specs,
+            out_specs=pl.BlockSpec((GROUP, width, width), lambda i, meta, table: (i, 0, 0)),
+        ),
+        compiler_params=pltpu.CompilerParams(vmem_limit_bytes=32 * 1024 * 1024),
+        name="multiply",
+    )(meta, table, *([held] * len(specs)))
+
+
+def device_meta(row, col):
+    devices, slots, _, _, _, _ = plan()
+    rows = []
+    for r, c in devices:
+        held = slots[(r, c)]
+        left = [held[(r, (c + w) % SIDE)] for w in range(STEPS)]
+        right, turned = [], []
+        for w in range(STEPS):
+            k = (c + w) % SIDE
+            right.append(held[(k, c)] if (k, c) in held else held[(c, k)])
+            turned.append(0 if (k, c) in held else 1)
+        rows.append([r, c] + left + right + turned)
+    return jnp.asarray(rows, jnp.int32)[row * SIDE + col]
+
+
+def square_per_device(values, partner):
+    table = lax.all_gather(partner[:, 0], ("row", "col")).reshape(-1)
+    meta = device_meta(lax.axis_index("row"), lax.axis_index("col"))
+    held = transported(values[:, 0])
+    return multiplied(held, meta, table)[:, None]
 
 
 def passed_along(value, axis, steps):
@@ -57,8 +391,9 @@
 
 
 def solution(mesh):
+    square = mesh.shape["row"] == SIDE and mesh.shape["col"] == SIDE
     return jax.shard_map(
-        per_device,
+        square_per_device if square else per_device,
         mesh=mesh,
         in_specs=(P(("groups", "row"), "col", None, None), P(("groups", "row"), "col")),
         out_specs=P(("groups", "row"), "col", None, None),

time: 959 us -> 436 us (0.45)
  waiting for transfers between devices: 821 us -> 0 us
  Pallas kernels: 0 us -> 418 us
  matrix products: 63.6 us -> 0 us
  local copies, waits for them, and re-layouts: 35.9 us -> 0.69 us
  between operations: 13.5 us -> 0.01 us
  other arithmetic: 11.2 us -> 0 us
  blocking collectives: 7.26 us -> 17.3 us
    psum x1 -> x0, waiting for transfers between devices: 643 us -> none  [spread(): return lax.psum(jnp.where(mine, value, jnp.zeros_like(value)), axis)]
    pallas_call x0 -> x2, Pallas kernels: none -> 418 us  [the longest x1 367 us: transported(): pl.pallas_call(transport_kernel, out_shape=jax.ShapeDtypeStruct((slot_cou...]
    ppermute x4 -> x0, waiting for transfers between devices: 178 us -> none  [passed_along(): return lax.ppermute(value, axis, pairs)]
    dot_general x3 -> x0, matrix products: 63.6 us -> none  [per_device(): jnp.einsum('nxy,nyz->nxz', carried_block, gathered, precision=lax.Precisi...]
    gather x6 -> x0, local copies, waits for them, and re-layouts: 26.9 us -> none  [the longest x3 23.2 us: per_device(): gathered = jnp.take(right_block, offsets, axis=0)]
    all_gather x0 -> x1, blocking collectives: none -> 17.3 us  [square_per_device(): table = lax.all_gather(partner[:, 0], ('row', 'col')).reshape(-1)]
    select_n x2 -> x0, other arithmetic: 11.2 us -> none  [spread(): return lax.psum(jnp.where(mine, value, jnp.zeros_like(value)), axis)]
  transfers between devices with their start and end apart: 5 -> 0, of which waited for: 4 -> 0; matrix products, arithmetic and copies ran while one was open for 7% -> 0% of each run, Pallas kernels for 0% -> 0%
where the time goes in v1:
time: 436 us
  Pallas kernels  418 us (96%)
  blocking collectives  17.3 us (4%)
    pallas_call x1, Pallas kernels, transported(): pl.pallas_call(transport_kernel, out_shape=jax.ShapeDtypeStruct((slot_cou...  367 us
    pallas_call x1, Pallas kernels, multiplied(): pl.pallas_call(functools.partial(product_kernel, size), out_shape=jax.Sha...  50.7 us
    all_gather x1, blocking collectives, square_per_device(): table = lax.all_gather(partner[:, 0], ('row', 'col')).reshape(-1)  17.3 us

profile of v1, /device:TPU:25, one launch (start us, length us, event | category | flops | bytes accessed | tf_op | source)
XLA Modules:
  0.0 435.5 jit_solution(8474545403895383075)
XLA Ops:
  0.0 0.7 dynamic-slice_bitcast_fusion.meta
  0.7 17.3 %all-gather = s32[2048,1]{0,1:T(1,128)S(1)} all-gather(s32[128,1]{0,1:T(1,128)} %param.4), channel_id=2, replica_groups=mesh['groups'=2,'row'=4,'col'=4] {'row','col'}, dimensions={0}, use_global_device_ids=true | all-gather | bytes 8704 | tf_op jit(solution)/shard_map/all_gather | solution.py:337
  18.0 366.8 %transport.1.refs_0_.refs_1_.refs_2_.refs_3_.refs_4_.refs_5_.refs_6_.refs_7_.refs_8_.refs_9_.refs_10_.refs_11_.refs_12_.refs_13_.refs_14_ = f32[6,128,128,128]{3,2,1,0:T(8,128)} custom-call(f32[128,128,128]{2,1,0:T(8,128)} %bitcast.8), custom_call_target="tpu_custom_call" | custom-call | tf_op jit(solution)/shard_map/transport/pallas_call | solution.py:236
  384.8 50.7 %multiply.1 = f32[128,128,128]{2,1,0:T(8,128)} custom-call(s32[11]{0:T(128)S(1)} %dynamic-slice_bitcast_fusion.meta, s32[2048]{0:T(1024)S(1)} %bitcast.7, f32[6,128,128,128]{3,2,1,0:T(8,128)} %transport.1.refs_0_.refs_1_.refs_2_.refs_3_.refs_4_.refs_5_.refs_6_.refs_7_.refs_8_.refs_9_.refs_10_.refs_11_.refs_12_.refs_13_.refs_14_, ...), custom_call_target="tpu_custom_call" | custom-call | tf_op jit(solution)/shard_map/multiply/pallas_call | solution.py:307

commit v2 on v0

--- a/solution.py
+++ b/solution.py
@@ -1,9 +1,406 @@
+import functools
 import jax
 import jax.numpy as jnp
 from jax import lax
+from jax.experimental import pallas as pl
+from jax.experimental.pallas import tpu as pltpu
 from jax.sharding import PartitionSpec as P
 
 STEPS = 3
+MESH = pl.DeviceIdType.MESH
+SIDE = 4
+HALVES = 2
+CHUNKS = 4
+GROUP = 8
+SLOT_LIMIT = 6
+
+FLOWS = (
+    (0, 0, 0, 1, 0, 1, 0, 0, 1, 0),
+    (0, 0, 0, 2, 0, 1, 1, 0, 1, 1),
+    (0, 1, 0, 2, 0, 2, 0, 0, 2, 0),
+    (0, 1, 0, 3, 0, 3, 0, 0, 3, 0),
+    (0, 1, 1, 1, 1, 1, 0, 1, 1, 0),
+    (0, 1, 1, 2, 1, 1, 1, 1, 1, 1),
+    (0, 1, 3, 1, 2, 1, 1, 2, 1, 1),
+    (0, 2, 0, 3, 0, 3, 0, 0, 3, 0),
+    (0, 2, 0, 0, 0, 0, 0, 0, 0, 0),
+    (0, 2, 2, 2, 1, 2, 1, 1, 2, 1),
+    (0, 2, 2, 3, 1, 2, 1, 1, 2, 1),
+    (0, 3, 0, 0, 0, 2, 1, 0, 2, 1),
+    (0, 3, 0, 1, 0, 1, 0, 0, 1, 0),
+    (0, 3, 3, 3, 1, 3, 2, 1, 3, 2),
+    (0, 3, 3, 1, 0, 1, 2, 0, 1, 2),
+    (1, 0, 1, 1, 1, 1, 0, 1, 1, 0),
+    (1, 0, 1, 2, 1, 1, 1, 1, 1, 1),
+    (1, 0, 0, 0, 0, 0, 0, 0, 0, 0),
+    (1, 0, 2, 0, 2, 0, 0, 2, 0, 0),
+    (1, 1, 1, 2, 1, 2, 0, 1, 2, 0),
+    (1, 1, 1, 3, 1, 2, 1, 1, 2, 1),
+    (1, 2, 1, 3, 1, 3, 0, 1, 3, 0),
+    (1, 2, 1, 0, 1, 0, 0, 1, 0, 0),
+    (1, 2, 2, 2, 2, 2, 0, 2, 2, 0),
+    (1, 2, 2, 3, 2, 3, 0, 2, 3, 0),
+    (1, 2, 0, 2, 0, 2, 0, 0, 2, 0),
+    (1, 3, 1, 0, 1, 2, 1, 1, 2, 1),
+    (1, 3, 1, 1, 1, 1, 0, 1, 1, 0),
+    (1, 3, 3, 3, 2, 3, 1, 2, 3, 1),
+    (1, 3, 0, 3, 0, 2, 1, 0, 2, 1),
+    (2, 0, 2, 1, 2, 1, 0, 2, 1, 0),
+    (2, 0, 2, 2, 2, 1, 1, 2, 1, 1),
+    (2, 0, 0, 0, 1, 0, 1, 1, 0, 1),
+    (2, 0, 0, 1, 3, 0, 1, 3, 0, 1),
+    (2, 1, 2, 2, 2, 2, 0, 2, 2, 0),
+    (2, 1, 2, 3, 2, 3, 0, 2, 3, 0),
+    (2, 1, 1, 1, 1, 0, 1, 1, 0, 1),
+    (2, 1, 3, 1, 3, 1, 0, 3, 1, 0),
+    (2, 2, 2, 3, 2, 3, 0, 2, 3, 0),
+    (2, 2, 2, 0, 2, 3, 1, 2, 3, 1),
+    (2, 3, 2, 0, 2, 0, 0, 2, 0, 0),
+    (2, 3, 2, 1, 2, 1, 0, 2, 1, 0),
+    (2, 3, 3, 3, 3, 3, 0, 3, 3, 0),
+    (2, 3, 3, 0, 3, 2, 2, 3, 2, 2),
+    (2, 3, 1, 3, 1, 3, 0, 1, 3, 0),
+    (3, 0, 3, 1, 3, 1, 0, 3, 1, 0),
+    (3, 0, 3, 2, 3, 1, 1, 3, 1, 1),
+    (3, 0, 0, 0, 2, 0, 2, 2, 0, 2),
+    (3, 0, 0, 1, 0, 1, 0, 0, 1, 0),
+    (3, 0, 2, 0, 3, 2, 2, 3, 2, 2),
+    (3, 1, 3, 2, 3, 2, 0, 3, 2, 0),
+    (3, 1, 3, 3, 3, 3, 0, 3, 3, 0),
+    (3, 1, 1, 1, 2, 1, 2, 2, 1, 2),
+    (3, 1, 2, 1, 2, 1, 0, 2, 1, 0),
+    (3, 2, 3, 3, 3, 3, 0, 3, 3, 0),
+    (3, 2, 3, 0, 3, 3, 1, 3, 3, 1),
+    (3, 2, 2, 2, 2, 2, 0, 2, 2, 0),
+    (3, 2, 2, 0, 2, 3, 1, 2, 3, 1),
+    (3, 3, 3, 0, 3, 0, 0, 3, 0, 0),
+    (3, 3, 3, 1, 3, 1, 0, 3, 1, 0),
+)
+
+
+def split_flows():
+    return [
+        ((f[0], f[1]), (f[2], f[3]), (((f[4], f[5]), f[6]), ((f[7], f[8]), f[9]))) for f in FLOWS
+    ]
+
+
+def plan():
+    devices = [(r, c) for r in range(SIDE) for c in range(SIDE)]
+    slots = {device: {device: 0} for device in devices}
+    for receiver, panel, _ in split_flows():
+        slots[receiver][panel] = len(slots[receiver])
+    slot_count = max(len(held) for held in slots.values())
+    tags = {device: [] for device in devices}
+    origins = {device: [None] * slot_count for device in devices}
+    for receiver, panel, _ in split_flows():
+        target = (slots[receiver][panel], receiver)
+        tags[panel].append(target)
+        origins[receiver][target[0]] = panel
+    halves_of = []
+    for half in range(HALVES):
+        sends = {device: [] for device in devices}
+        passed = {device: {} for device in devices}
+        senders = {device: [None] * slot_count for device in devices}
+        for receiver, panel, ways in split_flows():
+            sender, hops = ways[half]
+            target = (slots[receiver][panel], receiver)
+            senders[receiver][target[0]] = sender
+            if sender == panel:
+                sends[sender].append(target)
+            else:
+                step = passed[sender].setdefault(slots[sender][panel], (hops, []))
+                step[1].append(target)
+        steps = {
+            device: sorted((hops, slot, targets) for slot, (hops, targets) in passed[device].items())
+            for device in devices
+        }
+        halves_of.append((sends, steps, senders))
+    return devices, slots, slot_count, tags, origins, halves_of
+
+
+def encoded(target):
+    return -1 if target is None else (target[0] * SIDE + target[1][0]) * SIDE + target[1][1]
+
+
+def picked(me, table):
+    value = jnp.int32(table[0])
+    for position in range(1, len(table)):
+        if table[position] != table[0]:
+            value = jnp.where(me == position, jnp.int32(table[position]), value)
+    return value
+
+
+def padded(items, count):
+    return list(items) + [None] * (count - len(items))
+
+
+def transport_kernel(own_ref, tag_ref, held_ref, tags_ref, send_sem, recv_sem, tag_send, tag_recv, own_sem):
+    devices, _, slot_count, tags, origins, halves_of = plan()
+    group, row, col = lax.axis_index("groups"), lax.axis_index("row"), lax.axis_index("col")
+    me = row * SIDE + col
+    half_rows = own_ref.shape[0] // HALVES
+    chunk = half_rows // CHUNKS
+
+    def table(entry):
+        return picked(me, [encoded(entry(d)) for d in devices])
+
+    def listed(items):
+        count = max(len(items(d)) for d in devices)
+        return [table(lambda d: padded(items(d), count)[k]) for k in range(count)]
+
+    def places(items):
+        return [
+            table(lambda d: None if items(d)[slot] is None else (0, items(d)[slot]))
+            for slot in range(slot_count)
+        ]
+
+    tag_codes = listed(lambda d: tags[d])
+    origin_codes = places(lambda d: origins[d])
+    send_codes, step_slots, step_codes, sender_codes, last = [], [], [], [], []
+    for sends, steps, senders in halves_of:
+        send_codes.append(listed(lambda d: sends[d]))
+        sender_codes.append(places(lambda d: senders[d]))
+        step_count = max(len(steps[d]) for d in devices)
+
+        def step_at(d, k):
+            return steps[d][k] if k < len(steps[d]) else (0, -1, [])
+
+        step_slots.append(
+            [picked(me, [step_at(d, k)[1] for d in devices]) for k in range(step_count)]
+        )
+        step_codes.append([listed(lambda d: step_at(d, k)[2]) for k in range(step_count)])
+        last.append(
+            [
+                picked(
+                    me,
+                    [
+                        int(senders[d][slot] is not None and slot not in [t[1] for t in steps[d]])
+                        for d in devices
+                    ],
+                )
+                for slot in range(slot_count)
+            ]
+        )
+
+    def place(code):
+        return (group, code // SIDE % SIDE, code % SIDE)
+
+    barrier = pltpu.get_barrier_semaphore()
+    for codes in [origin_codes] + sender_codes:
+        for code in codes[1:]:
+            @pl.when(code >= 0)
+            def _():
+                pl.semaphore_signal(barrier, inc=1, device_id=place(code), device_id_type=MESH)
+    receivers = [
+        len(tags[d])
+        + sum(len(sends[d]) + sum(len(t[2]) for t in steps[d]) for sends, steps, _ in halves_of)
+        for d in devices
+    ]
+    pl.semaphore_wait(barrier, picked(me, receivers))
+
+    own_copy = pltpu.make_async_copy(own_ref, held_ref.at[0], own_sem.at[0])
+    own_tag = pltpu.make_async_copy(tag_ref, tags_ref.at[0], own_sem.at[1])
+
+    def tagged(code, index):
+        slot = code // (SIDE * SIDE)
+        return pltpu.make_async_remote_copy(
+            src_ref=tag_ref,
+            dst_ref=tags_ref.at[slot],
+            send_sem=tag_send.at[index],
+            recv_sem=tag_recv.at[slot],
+            device_id=place(code),
+            device_id_type=MESH,
+        )
+
+    def piece(half, q):
+        return pl.ds(half * half_rows + q * chunk, chunk)
+
+    def moved(source, slot, code, index, half, q):
+        return pltpu.make_async_remote_copy(
+            src_ref=source.at[piece(half, q)],
+            dst_ref=held_ref.at[slot, piece(half, q)],
+            send_sem=send_sem.at[half, index, q],
+            recv_sem=recv_sem.at[half, slot, q],
+            device_id=place(code),
+            device_id_type=MESH,
+        )
+
+    def arrived(slot, half, q):
+        moved(held_ref.at[slot], slot, me, 0, half, q).wait_recv()
+
+    for index, code in enumerate(tag_codes):
+        @pl.when(code >= 0)
+        def _():
+            tagged(code, index).start()
+    own_tag.start()
+
+    def start_own(q, carry):
+        for half in range(HALVES):
+            for index, code in enumerate(send_codes[half]):
+                @pl.when(code >= 0)
+                def _():
+                    moved(own_ref, code // (SIDE * SIDE), code, index, half, q).start()
+        return carry
+
+    lax.fori_loop(0, CHUNKS, start_own, 0)
+    own_copy.start()
+
+    def pass_on(q, carry):
+        for half in range(HALVES):
+            index = len(send_codes[half])
+            for slot, codes in zip(step_slots[half], step_codes[half]):
+                @pl.when(slot >= 0)
+                def _():
+                    arrived(slot, half, q)
+                for code in codes:
+                    @pl.when(code >= 0)
+                    def _():
+                        target = code // (SIDE * SIDE)
+                        moved(held_ref.at[slot], target, code, index, half, q).start()
+                    index += 1
+        return carry
+
+    lax.fori_loop(0, CHUNKS, pass_on, 0)
+
+    def finish(q, carry):
+        for half in range(HALVES):
+            for slot in range(1, slot_count):
+                @pl.when(last[half][slot] > 0)
+                def _():
+                    arrived(slot, half, q)
+            codes = send_codes[half] + [code for codes in step_codes[half] for code in codes]
+            for index, code in enumerate(codes):
+                @pl.when(code >= 0)
+                def _():
+                    moved(own_ref, 0, code, index, half, q).wait_send()
+        return carry
+
+    lax.fori_loop(0, CHUNKS, finish, 0)
+    for slot in range(1, slot_count):
+        @pl.when(origin_codes[slot] >= 0)
+        def _():
+            tagged(slot * SIDE * SIDE + me, 0).wait_recv()
+    for index, code in enumerate(tag_codes):
+        @pl.when(code >= 0)
+        def _():
+            tagged(code, index).wait_send()
+    own_tag.wait()
+    own_copy.wait()
+
+
+def transported(own_block, own_tags):
+    devices, _, slot_count, tags, _, halves_of = plan()
+    copies = 0
+    for sends, steps, _ in halves_of:
+        fans = [max((len(t[2]) for t in steps[d][k : k + 1]), default=0) for d in devices for k in range(SLOT_LIMIT)]
+        per_step = [max(fans[k::SLOT_LIMIT]) for k in range(SLOT_LIMIT)]
+        copies = max(copies, max(len(sends[d]) for d in devices) + sum(per_step))
+    return pl.pallas_call(
+        transport_kernel,
+        out_shape=(
+            jax.ShapeDtypeStruct((slot_count,) + own_block.shape, own_block.dtype),
+            jax.ShapeDtypeStruct((slot_count,) + own_tags.shape, own_tags.dtype),
+        ),
+        in_specs=[pl.BlockSpec(memory_space=pl.ANY)] * 2,
+        out_specs=(pl.BlockSpec(memory_space=pl.ANY),) * 2,
+        scratch_shapes=[
+            pltpu.SemaphoreType.DMA((HALVES, copies, CHUNKS)),
+            pltpu.SemaphoreType.DMA((HALVES, slot_count, CHUNKS)),
+            pltpu.SemaphoreType.DMA((max(len(tags[d]) for d in devices),)),
+            pltpu.SemaphoreType.DMA((slot_count,)),
+            pltpu.SemaphoreType.DMA((2,)),
+        ],
+        compiler_params=pltpu.CompilerParams(collective_id=0, has_side_effects=True),
+        name="transport",
+    )(own_block, own_tags)
+
+
+def halves(block):
+    high = block.astype(jnp.bfloat16)
+    return high, (block - high.astype(jnp.float32)).astype(jnp.bfloat16)
+
+
+def product_kernel(size, meta, table, *refs):
+    lefts = refs[:STEPS]
+    rights = refs[STEPS : 2 * STEPS]
+    out_ref = refs[-1]
+    col = meta[1]
+    for member in range(GROUP):
+        position = pl.program_id(0) * GROUP + member
+        target = table[position]
+        left_parts, right_parts = [], []
+        for window in range(STEPS):
+            turned = meta[8 + window] > 0
+            between = table[meta[2 + window] * size + position]
+            reach = between - lax.rem(col + window, SIDE) * size
+            place = jnp.where(turned, target - col * size, reach)
+            reached = table[meta[5 + window] * size + place]
+            matches = reached == jnp.where(turned, between, target)
+            left_high, left_low = halves(lefts[window][0, member])
+            block = rights[window][0, place]
+            block = lax.cond(turned, lambda b: b.T, lambda b: b, block)
+            block = jnp.where(matches, block, 0.0)
+            right_high, right_low = halves(block)
+            left_parts += [left_high, left_low, left_high]
+            right_parts += [right_high, right_high, right_low]
+        out_ref[member] = jnp.dot(
+            jnp.concatenate(left_parts, axis=1),
+            jnp.concatenate(right_parts, axis=0),
+            preferred_element_type=jnp.float32,
+        )
+
+
+def multiplied(held, meta, table):
+    size, width = held.shape[1], held.shape[2]
+
+    def left_spec(window):
+        return pl.BlockSpec(
+            (1, GROUP, width, width), lambda i, meta, table: (meta[2 + window], i, 0, 0)
+        )
+
+    def right_spec(window):
+        return pl.BlockSpec(
+            (1, size, width, width),
+            lambda i, meta, table: (meta[5 + window], 0, 0, 0),
+            pipeline_mode=pl.Buffered(1),
+        )
+
+    specs = [left_spec(w) for w in range(STEPS)] + [right_spec(w) for w in range(STEPS)]
+    return pl.pallas_call(
+        functools.partial(product_kernel, size),
+        out_shape=jax.ShapeDtypeStruct((size, width, width), jnp.float32),
+        grid_spec=pltpu.PrefetchScalarGridSpec(
+            num_scalar_prefetch=2,
+            grid=(size // GROUP,),
+            in_specs=specs,
+            out_specs=pl.BlockSpec((GROUP, width, width), lambda i, meta, table: (i, 0, 0)),
+        ),
+        compiler_params=pltpu.CompilerParams(vmem_limit_bytes=48 * 1024 * 1024),
+        name="multiply",
+    )(meta, table, *([held] * len(specs)))
+
+
+def device_meta(row, col):
+    devices, slots = plan()[:2]
+    rows = []
+    for r, c in devices:
+        held = slots[(r, c)]
+        left = [held[(r, (c + w) % SIDE)] for w in range(STEPS)]
+        right, turned = [], []
+        for w in range(STEPS):
+            k = (c + w) % SIDE
+            right.append(held[(k, c)] if (k, c) in held else held[(c, k)])
+            turned.append(0 if (k, c) in held else 1)
+        rows.append([r, c] + left + right + turned)
+    return jnp.asarray(rows, jnp.int32)[row * SIDE + col]
+
+
+def square_per_device(values, partner):
+    size = partner.shape[0]
+    meta = device_meta(lax.axis_index("row"), lax.axis_index("col"))
+    tags = jnp.broadcast_to(partner[:, 0][None, :], (8, size))
+    held, held_tags = transported(values[:, 0], tags)
+    return multiplied(held, meta, held_tags[:, 0, :].reshape(-1))[:, None]
 
 
 def passed_along(value, axis, steps):
@@ -57,8 +454,9 @@
 
 
 def solution(mesh):
+    square = mesh.shape["row"] == SIDE and mesh.shape["col"] == SIDE
     return jax.shard_map(
-        per_device,
+        square_per_device if square else per_device,
         mesh=mesh,
         in_specs=(P(("groups", "row"), "col", None, None), P(("groups", "row"), "col")),
         out_specs=P(("groups", "row"), "col", None, None),

time: 959 us -> 414 us (0.43)
  waiting for transfers between devices: 821 us -> 0 us
  Pallas kernels: 0 us -> 411 us
  matrix products: 63.6 us -> 0 us
  local copies, waits for them, and re-layouts: 35.9 us -> 2.69 us
  between operations: 13.5 us -> 0.01 us
  other arithmetic: 11.2 us -> 0 us
    psum x1 -> x0, waiting for transfers between devices: 643 us -> none  [spread(): return lax.psum(jnp.where(mine, value, jnp.zeros_like(value)), axis)]
    pallas_call x0 -> x2, Pallas kernels: none -> 411 us  [the longest x1 364 us: transported(): pl.pallas_call(transport_kernel, out_shape=(jax.ShapeDtypeStruct((slot_co...]
    ppermute x4 -> x0, waiting for transfers between devices: 178 us -> none  [passed_along(): return lax.ppermute(value, axis, pairs)]
    dot_general x3 -> x0, matrix products: 63.6 us -> none  [per_device(): jnp.einsum('nxy,nyz->nxz', carried_block, gathered, precision=lax.Precisi...]
    gather x6 -> x0, local copies, waits for them, and re-layouts: 26.9 us -> none  [the longest x3 23.2 us: per_device(): gathered = jnp.take(right_block, offsets, axis=0)]
    select_n x2 -> x0, other arithmetic: 11.2 us -> none  [spread(): return lax.psum(jnp.where(mine, value, jnp.zeros_like(value)), axis)]
  transfers between devices with their start and end apart: 5 -> 0, of which waited for: 4 -> 0; matrix products, arithmetic and copies ran while one was open for 7% -> 0% of each run, Pallas kernels for 0% -> 0%
where the time goes in v2:
time: 414 us
  Pallas kernels  411 us (99%)
    pallas_call x1, Pallas kernels, transported(): pl.pallas_call(transport_kernel, out_shape=(jax.ShapeDtypeStruct((slot_co...  364 us
    pallas_call x1, Pallas kernels, multiplied(): pl.pallas_call(functools.partial(product_kernel, size), out_shape=jax.Sha...  47.3 us

profile of v2, /device:TPU:25, one launch (start us, length us, event | category | flops | bytes accessed | tf_op | source)
XLA Modules:
  0.0 413.8 jit_solution(3491288974604818341)
XLA Ops:
  0.0 0.7 dynamic-slice_bitcast_fusion.meta
  0.7 1.2 broadcast_in_dim.11.tag_ref
  1.9 363.8 %transport.1 = (f32[6,128,128,128]{3,2,1,0:T(8,128)}, s32[6,8,128]{2,1,0:T(8,128)}) custom-call(f32[128,128,128]{2,1,0:T(8,128)} %bitcast.9, s32[8,128]{1,0:T(8,128)} %broadcast_in_dim.11.tag_ref), custom_call_target="tpu_custom_call" | custom-call | tf_op jit(solution)/shard_map/transport/pallas_call | solution.py:298
  365.7 0.7 slice_reduce_fusion
  366.5 47.3 %multiply.1 = f32[128,128,128]{2,1,0:T(8,128)} custom-call(s32[11]{0:T(128)S(1)} %dynamic-slice_bitcast_fusion.meta, s32[768]{0:T(1024)S(1)} %bitcast.8, f32[6,128,128,128]{3,2,1,0:T(8,128)} %get-tuple-element.8.refs_0_.refs_1_.refs_2_.refs_3_.refs_4_.refs_5_, f32[6,128,128,128]{3,2,1,0:T(8,128)} %get-tuple-element.8.refs_0_.refs_1_.refs_2_.refs_3_.refs_4_.refs_5_, ...), custom_call_target="tpu_custom_call" | custom-call | tf_op jit(solution)/shard_map/multiply/pallas_call | solution.py:369

commit v3 on v2

--- a/solution.py
+++ b/solution.py
@@ -16,8 +16,8 @@
 
 FLOWS = (
     (0, 0, 0, 1, 0, 1, 0, 0, 1, 0),
-    (0, 0, 0, 2, 0, 1, 1, 0, 1, 1),
-    (0, 1, 0, 2, 0, 2, 0, 0, 2, 0),
+    (0, 0, 0, 2, 0, 2, 0, 0, 2, 0),
+    (0, 1, 0, 2, 0, 0, 1, 0, 0, 1),
     (0, 1, 0, 3, 0, 3, 0, 0, 3, 0),
     (0, 1, 1, 1, 1, 1, 0, 1, 1, 0),
     (0, 1, 1, 2, 1, 1, 1, 1, 1, 1),
@@ -28,37 +28,37 @@
     (0, 2, 2, 3, 1, 2, 1, 1, 2, 1),
     (0, 3, 0, 0, 0, 2, 1, 0, 2, 1),
     (0, 3, 0, 1, 0, 1, 0, 0, 1, 0),
-    (0, 3, 3, 3, 1, 3, 2, 1, 3, 2),
+    (0, 3, 3, 3, 1, 3, 2, 1, 3, 1),
     (0, 3, 3, 1, 0, 1, 2, 0, 1, 2),
     (1, 0, 1, 1, 1, 1, 0, 1, 1, 0),
     (1, 0, 1, 2, 1, 1, 1, 1, 1, 1),
     (1, 0, 0, 0, 0, 0, 0, 0, 0, 0),
     (1, 0, 2, 0, 2, 0, 0, 2, 0, 0),
     (1, 1, 1, 2, 1, 2, 0, 1, 2, 0),
-    (1, 1, 1, 3, 1, 2, 1, 1, 2, 1),
+    (1, 1, 1, 3, 1, 3, 0, 1, 3, 0),
     (1, 2, 1, 3, 1, 3, 0, 1, 3, 0),
-    (1, 2, 1, 0, 1, 0, 0, 1, 0, 0),
+    (1, 2, 1, 0, 1, 0, 0, 1, 3, 1),
     (1, 2, 2, 2, 2, 2, 0, 2, 2, 0),
     (1, 2, 2, 3, 2, 3, 0, 2, 3, 0),
     (1, 2, 0, 2, 0, 2, 0, 0, 2, 0),
-    (1, 3, 1, 0, 1, 2, 1, 1, 2, 1),
+    (1, 3, 1, 0, 1, 2, 1, 1, 0, 0),
     (1, 3, 1, 1, 1, 1, 0, 1, 1, 0),
-    (1, 3, 3, 3, 2, 3, 1, 2, 3, 1),
-    (1, 3, 0, 3, 0, 2, 1, 0, 2, 1),
+    (1, 3, 3, 3, 2, 3, 1, 3, 3, 0),
+    (1, 3, 0, 3, 0, 3, 0, 0, 3, 0),
     (2, 0, 2, 1, 2, 1, 0, 2, 1, 0),
-    (2, 0, 2, 2, 2, 1, 1, 2, 1, 1),
+    (2, 0, 2, 2, 2, 1, 1, 2, 2, 0),
     (2, 0, 0, 0, 1, 0, 1, 1, 0, 1),
     (2, 0, 0, 1, 3, 0, 1, 3, 0, 1),
-    (2, 1, 2, 2, 2, 2, 0, 2, 2, 0),
+    (2, 1, 2, 2, 2, 2, 0, 2, 0, 1),
     (2, 1, 2, 3, 2, 3, 0, 2, 3, 0),
-    (2, 1, 1, 1, 1, 0, 1, 1, 0, 1),
+    (2, 1, 1, 1, 1, 1, 0, 1, 1, 0),
     (2, 1, 3, 1, 3, 1, 0, 3, 1, 0),
     (2, 2, 2, 3, 2, 3, 0, 2, 3, 0),
     (2, 2, 2, 0, 2, 3, 1, 2, 3, 1),
     (2, 3, 2, 0, 2, 0, 0, 2, 0, 0),
     (2, 3, 2, 1, 2, 1, 0, 2, 1, 0),
     (2, 3, 3, 3, 3, 3, 0, 3, 3, 0),
-    (2, 3, 3, 0, 3, 2, 2, 3, 2, 2),
+    (2, 3, 0, 3, 1, 3, 1, 1, 3, 1),
     (2, 3, 1, 3, 1, 3, 0, 1, 3, 0),
     (3, 0, 3, 1, 3, 1, 0, 3, 1, 0),
     (3, 0, 3, 2, 3, 1, 1, 3, 1, 1),
@@ -67,14 +67,15 @@
     (3, 0, 2, 0, 3, 2, 2, 3, 2, 2),
     (3, 1, 3, 2, 3, 2, 0, 3, 2, 0),
     (3, 1, 3, 3, 3, 3, 0, 3, 3, 0),
-    (3, 1, 1, 1, 2, 1, 2, 2, 1, 2),
-    (3, 1, 2, 1, 2, 1, 0, 2, 1, 0),
+    (3, 1, 1, 1, 2, 1, 1, 2, 1, 1),
+    (3, 1, 2, 1, 2, 1, 0, 3, 3, 2),
     (3, 2, 3, 3, 3, 3, 0, 3, 3, 0),
-    (3, 2, 3, 0, 3, 3, 1, 3, 3, 1),
+    (3, 2, 3, 0, 3, 0, 0, 3, 0, 0),
     (3, 2, 2, 2, 2, 2, 0, 2, 2, 0),
     (3, 2, 2, 0, 2, 3, 1, 2, 3, 1),
-    (3, 3, 3, 0, 3, 0, 0, 3, 0, 0),
+    (3, 3, 3, 0, 3, 2, 1, 3, 2, 1),
     (3, 3, 3, 1, 3, 1, 0, 3, 1, 0),
+    (3, 3, 2, 1, -1, -1, 0, 2, 3, 1),
 )
 
 
@@ -103,6 +104,8 @@
         senders = {device: [None] * slot_count for device in devices}
         for receiver, panel, ways in split_flows():
             sender, hops = ways[half]
+            if sender not in devices:
+                continue
             target = (slots[receiver][panel], receiver)
             senders[receiver][target[0]] = sender
             if sender == panel:
@@ -341,13 +344,16 @@
             block = lax.cond(turned, lambda b: b.T, lambda b: b, block)
             block = jnp.where(matches, block, 0.0)
             right_high, right_low = halves(block)
-            left_parts += [left_high, left_low, left_high]
-            right_parts += [right_high, right_high, right_low]
-        out_ref[member] = jnp.dot(
+            left_parts.append(jnp.concatenate([left_high, left_low], axis=0))
+            right_parts.append(jnp.concatenate([right_high, right_low], axis=1))
+        parts = jnp.dot(
             jnp.concatenate(left_parts, axis=1),
             jnp.concatenate(right_parts, axis=0),
             preferred_element_type=jnp.float32,
         )
+        width = out_ref.shape[-1]
+        small = parts[:width, width:] + parts[width:, :width] + parts[width:, width:]
+        out_ref[member] = parts[:width, :width] + small
 
 
 def multiplied(held, meta, table):

time: 414 us -> 414 us (level)
  the two profiles are of different devices: /device:TPU:25 before, /device:TPU:7 now
where the time goes in v3:
time: 414 us
  Pallas kernels  412 us (100%)
    pallas_call x1, Pallas kernels, transported(): pl.pallas_call(transport_kernel, out_shape=(jax.ShapeDtypeStruct((slot_co...  347 us
    pallas_call x1, Pallas kernels, multiplied(): pl.pallas_call(functools.partial(product_kernel, size), out_shape=jax.Sha...  64.8 us

profile of v3, /device:TPU:7, one launch (start us, length us, event | category | flops | bytes accessed | tf_op | source)
XLA Modules:
  0.0 414.3 jit_solution(1711014301199307392)
XLA Ops:
  0.0 0.7 dynamic-slice_bitcast_fusion.meta
  0.7 1.2 broadcast_in_dim.11.tag_ref
  1.9 346.8 %transport.1 = (f32[6,128,128,128]{3,2,1,0:T(8,128)}, s32[6,8,128]{2,1,0:T(8,128)}) custom-call(f32[128,128,128]{2,1,0:T(8,128)} %bitcast.9, s32[8,128]{1,0:T(8,128)} %broadcast_in_dim.11.tag_ref), custom_call_target="tpu_custom_call" | custom-call | tf_op jit(solution)/shard_map/transport/pallas_call | solution.py:301
  348.8 0.7 slice_reduce_fusion
  349.5 64.8 %multiply.1 = f32[128,128,128]{2,1,0:T(8,128)} custom-call(s32[11]{0:T(128)S(1)} %dynamic-slice_bitcast_fusion.meta, s32[768]{0:T(1024)S(1)} %bitcast.8, f32[6,128,128,128]{3,2,1,0:T(8,128)} %get-tuple-element.8.refs_0_.refs_1_.refs_2_.refs_3_.refs_4_.refs_5_, f32[6,128,128,128]{3,2,1,0:T(8,128)} %get-tuple-element.8.refs_0_.refs_1_.refs_2_.refs_3_.refs_4_.refs_5_, ...), custom_call_target="tpu_custom_call" | custom-call | tf_op jit(solution)/shard_map/multiply/pallas_call | solution.py:375

commit v4 on v2

--- a/solution.py
+++ b/solution.py
@@ -68,13 +68,14 @@
     (3, 1, 3, 2, 3, 2, 0, 3, 2, 0),
     (3, 1, 3, 3, 3, 3, 0, 3, 3, 0),
     (3, 1, 1, 1, 2, 1, 2, 2, 1, 2),
-    (3, 1, 2, 1, 2, 1, 0, 2, 1, 0),
+    (3, 1, 2, 1, 2, 1, 0, 3, 3, 2),
     (3, 2, 3, 3, 3, 3, 0, 3, 3, 0),
     (3, 2, 3, 0, 3, 3, 1, 3, 3, 1),
     (3, 2, 2, 2, 2, 2, 0, 2, 2, 0),
     (3, 2, 2, 0, 2, 3, 1, 2, 3, 1),
     (3, 3, 3, 0, 3, 0, 0, 3, 0, 0),
     (3, 3, 3, 1, 3, 1, 0, 3, 1, 0),
+    (3, 3, 2, 1, -1, -1, 0, 2, 3, 1),
 )
 
 
@@ -103,6 +104,8 @@
         senders = {device: [None] * slot_count for device in devices}
         for receiver, panel, ways in split_flows():
             sender, hops = ways[half]
+            if sender not in devices:
+                continue
             target = (slots[receiver][panel], receiver)
             senders[receiver][target[0]] = sender
             if sender == panel:
@@ -325,29 +328,36 @@
     rights = refs[STEPS : 2 * STEPS]
     out_ref = refs[-1]
     col = meta[1]
-    for member in range(GROUP):
-        position = pl.program_id(0) * GROUP + member
-        target = table[position]
-        left_parts, right_parts = [], []
-        for window in range(STEPS):
-            turned = meta[8 + window] > 0
-            between = table[meta[2 + window] * size + position]
-            reach = between - lax.rem(col + window, SIDE) * size
-            place = jnp.where(turned, target - col * size, reach)
-            reached = table[meta[5 + window] * size + place]
-            matches = reached == jnp.where(turned, between, target)
-            left_high, left_low = halves(lefts[window][0, member])
-            block = rights[window][0, place]
-            block = lax.cond(turned, lambda b: b.T, lambda b: b, block)
-            block = jnp.where(matches, block, 0.0)
-            right_high, right_low = halves(block)
-            left_parts += [left_high, left_low, left_high]
-            right_parts += [right_high, right_high, right_low]
-        out_ref[member] = jnp.dot(
-            jnp.concatenate(left_parts, axis=1),
-            jnp.concatenate(right_parts, axis=0),
-            preferred_element_type=jnp.float32,
-        )
+
+    def members(turned):
+        for member in range(GROUP):
+            position = pl.program_id(0) * GROUP + member
+            target = table[position]
+            left_parts, right_parts = [], []
+            for window in range(STEPS):
+                between = table[meta[2 + window] * size + position]
+                if turned[window]:
+                    place, wanted = target - col * size, between
+                else:
+                    place, wanted = between - lax.rem(col + window, SIDE) * size, target
+                matches = table[meta[5 + window] * size + place] == wanted
+                left_high, left_low = halves(lefts[window][0, member])
+                block = rights[window][0, place]
+                block = block.T if turned[window] else block
+                right_high, right_low = halves(jnp.where(matches, block, 0.0))
+                left_parts += [left_high, left_low, left_high]
+                right_parts += [right_high, right_high, right_low]
+            out_ref[member] = jnp.dot(
+                jnp.concatenate(left_parts, axis=1),
+                jnp.concatenate(right_parts, axis=0),
+                preferred_element_type=jnp.float32,
+            )
+
+    for second in (False, True):
+        for third in (False, True):
+            @pl.when(jnp.logical_and(meta[9] == int(second), meta[10] == int(third)))
+            def _():
+                members((False, second, third))
 
 
 def multiplied(held, meta, table):

time: 414 us -> 353 us (0.85)
  Pallas kernels: 411 us -> 349 us
    pallas_call x1, Pallas kernels: 364 us -> 320 us  [transported(): pl.pallas_call(transport_kernel, out_shape=(jax.ShapeDtypeStruct((slot_co...]
    pallas_call x1, Pallas kernels: 47.3 us -> 29.5 us  [multiplied(): pl.pallas_call(functools.partial(product_kernel, size), out_shape=jax.Sha...]
where the time goes in v4:
time: 353 us; the launch traced here: 352 us
  Pallas kernels  349 us (99%)
    pallas_call x1, Pallas kernels, transported(): pl.pallas_call(transport_kernel, out_shape=(jax.ShapeDtypeStruct((slot_co...  320 us
    pallas_call x1, Pallas kernels, multiplied(): pl.pallas_call(functools.partial(product_kernel, size), out_shape=jax.Sha...  29.5 us

profile of v4, /device:TPU:25, one launch (start us, length us, event | category | flops | bytes accessed | tf_op | source)
XLA Modules:
  0.0 351.9 jit_solution(11859484018084471683)
XLA Ops:
  0.0 0.7 dynamic-slice_bitcast_fusion.meta
  0.7 1.2 broadcast_in_dim.11.tag_ref
  1.9 319.7 %transport.1 = (f32[6,128,128,128]{3,2,1,0:T(8,128)}, s32[6,8,128]{2,1,0:T(8,128)}) custom-call(f32[128,128,128]{2,1,0:T(8,128)} %bitcast.9, s32[8,128]{1,0:T(8,128)} %broadcast_in_dim.11.tag_ref), custom_call_target="tpu_custom_call" | custom-call | tf_op jit(solution)/shard_map/transport/pallas_call | solution.py:301
  321.7 0.7 slice_reduce_fusion
  322.4 29.5 %multiply.1 = f32[128,128,128]{2,1,0:T(8,128)} custom-call(s32[11]{0:T(128)S(1)} %dynamic-slice_bitcast_fusion.meta, s32[768]{0:T(1024)S(1)} %bitcast.8, f32[6,128,128,128]{3,2,1,0:T(8,128)} %get-tuple-element.8.refs_0_.refs_1_.refs_2_.refs_3_.refs_4_.refs_5_, f32[6,128,128,128]{3,2,1,0:T(8,128)} %get-tuple-element.8.refs_0_.refs_1_.refs_2_.refs_3_.refs_4_.refs_5_, ...), custom_call_target="tpu_custom_call" | custom-call | tf_op jit(solution)/shard_map/multiply/pallas_call | solution.py:379

commit v5 on v4

--- a/solution.py
+++ b/solution.py
@@ -10,7 +10,7 @@
 MESH = pl.DeviceIdType.MESH
 SIDE = 4
 HALVES = 2
-CHUNKS = 4
+CHUNKS = 8
 GROUP = 8
 SLOT_LIMIT = 6
 

time: 353 us -> 354 us (level)
  no operation moved by 1% of the time
where the time goes in v5:
time: 354 us; the launch traced here: 353 us
  Pallas kernels  350 us (99%)
    pallas_call x1, Pallas kernels, transported(): pl.pallas_call(transport_kernel, out_shape=(jax.ShapeDtypeStruct((slot_co...  321 us
    pallas_call x1, Pallas kernels, multiplied(): pl.pallas_call(functools.partial(product_kernel, size), out_shape=jax.Sha...  29.5 us

profile of v5, /device:TPU:25, one launch (start us, length us, event | category | flops | bytes accessed | tf_op | source)
XLA Modules:
  0.0 352.9 jit_solution(3404464450110968805)
XLA Ops:
  0.0 0.7 dynamic-slice_bitcast_fusion.meta
  0.7 1.2 broadcast_in_dim.11.tag_ref
  1.9 320.7 %transport.1 = (f32[6,128,128,128]{3,2,1,0:T(8,128)}, s32[6,8,128]{2,1,0:T(8,128)}) custom-call(f32[128,128,128]{2,1,0:T(8,128)} %bitcast.9, s32[8,128]{1,0:T(8,128)} %broadcast_in_dim.11.tag_ref), custom_call_target="tpu_custom_call" | custom-call | tf_op jit(solution)/shard_map/transport/pallas_call | solution.py:301
  322.7 0.7 slice_reduce_fusion
  323.4 29.5 %multiply.1 = f32[128,128,128]{2,1,0:T(8,128)} custom-call(s32[11]{0:T(128)S(1)} %dynamic-slice_bitcast_fusion.meta, s32[768]{0:T(1024)S(1)} %bitcast.8, f32[6,128,128,128]{3,2,1,0:T(8,128)} %get-tuple-element.8.refs_0_.refs_1_.refs_2_.refs_3_.refs_4_.refs_5_, f32[6,128,128,128]{3,2,1,0:T(8,128)} %get-tuple-element.8.refs_0_.refs_1_.refs_2_.refs_3_.refs_4_.refs_5_, ...), custom_call_target="tpu_custom_call" | custom-call | tf_op jit(solution)/shard_map/multiply/pallas_call | solution.py:379

commit v6 on v4

--- a/solution.py
+++ b/solution.py
@@ -11,7 +11,7 @@
 SIDE = 4
 HALVES = 2
 CHUNKS = 4
-GROUP = 8
+GROUP = 16
 SLOT_LIMIT = 6
 
 FLOWS = (

time: 353 us -> 349 us (0.989)
    pallas_call x1, Pallas kernels: 29.5 us -> 25.9 us  [multiplied(): pl.pallas_call(functools.partial(product_kernel, size), out_shape=jax.Sha...]
where the time goes in v6:
time: 349 us; the launch traced here: 348 us
  Pallas kernels  346 us (99%)
    pallas_call x1, Pallas kernels, transported(): pl.pallas_call(transport_kernel, out_shape=(jax.ShapeDtypeStruct((slot_co...  320 us
    pallas_call x1, Pallas kernels, multiplied(): pl.pallas_call(functools.partial(product_kernel, size), out_shape=jax.Sha...  25.9 us

profile of v6, /device:TPU:25, one launch (start us, length us, event | category | flops | bytes accessed | tf_op | source)
XLA Modules:
  0.0 348.3 jit_solution(7100893061320200761)
XLA Ops:
  0.0 0.7 dynamic-slice_bitcast_fusion.meta
  0.7 1.2 broadcast_in_dim.11.tag_ref
  1.9 319.7 %transport.1 = (f32[6,128,128,128]{3,2,1,0:T(8,128)}, s32[6,8,128]{2,1,0:T(8,128)}) custom-call(f32[128,128,128]{2,1,0:T(8,128)} %bitcast.9, s32[8,128]{1,0:T(8,128)} %broadcast_in_dim.11.tag_ref), custom_call_target="tpu_custom_call" | custom-call | tf_op jit(solution)/shard_map/transport/pallas_call | solution.py:301
  321.7 0.7 slice_reduce_fusion
  322.4 25.9 %multiply.1 = f32[128,128,128]{2,1,0:T(8,128)} custom-call(s32[11]{0:T(128)S(1)} %dynamic-slice_bitcast_fusion.meta, s32[768]{0:T(1024)S(1)} %bitcast.8, f32[6,128,128,128]{3,2,1,0:T(8,128)} %get-tuple-element.8.refs_0_.refs_1_.refs_2_.refs_3_.refs_4_.refs_5_, f32[6,128,128,128]{3,2,1,0:T(8,128)} %get-tuple-element.8.refs_0_.refs_1_.refs_2_.refs_3_.refs_4_.refs_5_, ...), custom_call_target="tpu_custom_call" | custom-call | tf_op jit(solution)/shard_map/multiply/pallas_call | solution.py:379
